TPU v7x, 768 devices: a whole 4x8x12 slice. The times are simulated.
768 devices in a mesh: row: 96 (over z, x, core), col: 8 (over y).
Axes of the slice: x: 4, y: 8, z: 12, core: 2. Of those that a mesh axis runs over, the one named last changes fastest.
Arguments:
- ensemble: float32 [98304, 1024], P(('row', 'col')), may hold values from -6 to 6
- obs_blocks: int32 [2, 256], replicated, may hold values from 0 to 24575
- obs_weights: float32 [2, 256, 4], replicated, may hold values from 0.1 to 1
- comp_tags: int32 [2, 256], replicated, may hold values from 0 to 1
- obs_values: float32 [2, 256], replicated, may hold values from -6 to 6
- obs_noise: bfloat16 [2, 256, 1024], replicated, may hold values from -6 to 6
Outputs:
- analysis: float32 [98304, 1024], P(('row', 'col'))
Inputs may be any that keep to these rules, and one draw needn't show every extreme that they name: Observation o reads state rows 4 * obs_blocks[b, o] to 4 * obs_blocks[b, o] + 3. `comp_tags`: 0 marks an atmosphere observation, 1 an ocean one.
All inputs are finite; a program needn't handle non-finite values.
Results may differ from a plain program's by a relative error of at most 0.0035.
Values may be sent and summed in bfloat16 or wider, within the bound.
A program may use at most 32 MiB of HBM per device.

v0:
```python
import functools

import jax
import jax.numpy as jnp
from jax import lax
from jax.experimental import pallas as pl
from jax.experimental.pallas import tpu as pltpu
from jax.sharding import PartitionSpec as P

NX = 4
TILE_ROWS = 16
TILE_COLS = 128
MESH = pl.DeviceIdType.MESH


def split(value):
    high = value.astype(jnp.bfloat16)
    return high, (value - high.astype(jnp.float32)).astype(jnp.bfloat16)


def dot_tn(left, right):
    return lax.dot_general(
        left, right, (((0,), (0,)), ((), ())), preferred_element_type=jnp.float32
    )


def gather_kernel(nz, nx, ny, state_ref, blocks_ref, weights_ref, out_ref, *scratch):
    nb = blocks_ref.shape[0]
    batches = [scratch[7 * b : 7 * b + 7] for b in range(nb)]
    send_sems, recv_sems = scratch[7 * nb :]
    row = lax.axis_index("row")
    y = lax.axis_index("col")
    core = lax.rem(row, 2)
    x = lax.rem(row // 2, nx)
    z = row // (2 * nx)

    def place(z_, x_, core_, y_):
        return ((z_ * nx + x_) * 2 + core_, y_)

    core_peer = place(z, x, 1 - core, y)
    x_peers = [place(z, lax.rem(x + d, nx), core, y) for d in range(1, nx)]
    y_peers = [place(z, x, core, lax.rem(y + d, ny)) for d in range(1, ny)]
    z_peers = [place(lax.rem(z + d, nz), x, core, y) for d in range(1, nz)]
    peers = [core_peer, *x_peers, *y_peers, *z_peers]

    barrier = pltpu.get_barrier_semaphore()
    for peer in peers:
        pl.semaphore_signal(barrier, inc=1, device_id=peer, device_id_type=MESH)

    def interpolate(b):
        part = batches[b][0]
        rows = state_ref.shape[0]
        state_high, state_low = split(state_ref[...])
        observations = blocks_ref.shape[1]
        position = lax.broadcasted_iota(jnp.int32, (rows, observations), 0)
        first = (row * ny + y) * (rows // 4)
        held = blocks_ref[b : b + 1, :] - first == position // 4
        within = lax.rem(position, 4)
        weights = jnp.zeros((rows, observations), jnp.float32)
        for k in range(4):
            weights = jnp.where(within == k, weights_ref[b, k : k + 1, :], weights)
        selector_high, selector_low = split(jnp.where(held, weights, 0.0))
        values = (
            dot_tn(selector_low, state_high)
            + dot_tn(selector_high, state_low)
            + dot_tn(selector_high, state_high)
        ).astype(jnp.bfloat16)
        tile = 0
        per_x = part.shape[1] // nx
        half = part.shape[1]
        for i in range(values.shape[0] // TILE_ROWS):
            for j in range(values.shape[1] // TILE_COLS):
                part[tile // half, tile % half] = values[
                    i * TILE_ROWS : (i + 1) * TILE_ROWS, j * TILE_COLS : (j + 1) * TILE_COLS
                ]
                tile += 1

    def copy(b, index, source, target, peer):
        return pltpu.make_async_remote_copy(
            src_ref=source,
            dst_ref=target,
            send_sem=send_sems.at[b, index],
            recv_sem=recv_sems.at[b, index],
            device_id=peer,
            device_id_type=MESH,
        )

    per_x = batches[0][0].shape[1] // nx
    per_y = per_x // ny
    base = [0]
    for count in (1, nx - 1, ny - 1, nz - 1, ny - 1, nx - 1, 1):
        base.append(base[-1] + count)

    def start_stage(b, stage):
        part, from_core, from_x, from_y, from_z, mine, full = batches[b]
        copies = []
        if stage == 0:
            copies.append(copy(b, 0, part.at[1 - core], from_core, core_peer))
        elif stage == 1:
            for d in range(1, nx):
                target = lax.rem(x + d, nx)
                source = part.at[core, pl.ds(target * per_x, per_x)]
                copies.append(copy(b, base[1] + d - 1, source, from_x.at[d - 1], x_peers[d - 1]))
        elif stage == 2:
            for d in range(1, ny):
                target = lax.rem(y + d, ny)
                source = part.at[core, pl.ds(x * per_x + target * per_y, per_y)]
                copies.append(copy(b, base[2] + d - 1, source, from_y.at[d - 1], y_peers[d - 1]))
        elif stage == 3:
            for d in range(1, nz):
                copies.append(copy(b, base[3] + d - 1, mine, from_z.at[d - 1], z_peers[d - 1]))
        elif stage == 4:
            whole = full.at[core, x, y]
            for d in range(1, ny):
                copies.append(copy(b, base[4] + d - 1, whole, whole, y_peers[d - 1]))
        elif stage == 5:
            whole = full.at[core, x]
            for d in range(1, nx):
                copies.append(copy(b, base[5] + d - 1, whole, whole, x_peers[d - 1]))
        else:
            whole = full.at[core]
            copies.append(copy(b, base[6], whole, whole, core_peer))
        for each in copies:
            each.start()
        return copies

    def finish_stage(b, stage, copies):
        part, from_core, from_x, from_y, from_z, mine, full = batches[b]
        for each in copies:
            each.wait_recv()
        if stage == 0:
            part[core] = part[core] + from_core[...]
        elif stage == 1:
            here = pl.ds(x * per_x, per_x)
            part[core, here] = part[core, here] + functools.reduce(
                jnp.add, [from_x[d] for d in range(nx - 1)]
            )
        elif stage == 2:
            here = pl.ds(x * per_x + y * per_y, per_y)
            mine[...] = part[core, here] + functools.reduce(
                jnp.add, [from_y[d] for d in range(ny - 1)]
            )
        elif stage == 3:
            full[core, x, y] = mine[...] + functools.reduce(
                jnp.add, [from_z[d] for d in range(nz - 1)]
            )

    started = [[] for _ in range(nb)]
    current = [None] * nb
    for b in range(nb):
        interpolate(b)
        if b == 0:
            pl.semaphore_wait(barrier, len(peers))
        current[b] = start_stage(b, 0)
        started[b] += current[b]
    for stage in range(7):
        for b in range(nb):
            finish_stage(b, stage, current[b])
            if stage < 6:
                current[b] = start_stage(b, stage + 1)
                started[b] += current[b]
    for b in range(nb):
        full = batches[b][6]
        columns = out_ref.shape[2] // TILE_COLS
        for i in range(out_ref.shape[1] // TILE_ROWS):
            for j in range(columns):
                tile = i * columns + j
                c, rest = divmod(tile, nx * per_x)
                x_, rest = divmod(rest, per_x)
                y_, t = divmod(rest, per_y)
                out_ref[
                    b, i * TILE_ROWS : (i + 1) * TILE_ROWS, j * TILE_COLS : (j + 1) * TILE_COLS
                ] = full[c, x_, y_, t]
    for b in range(nb):
        for each in started[b]:
            each.wait_send()


def gather_observed(ensemble, obs_blocks, obs_weights):
    nx = NX
    ny = lax.axis_size("col")
    nz = lax.axis_size("row") // (2 * nx)
    batches, observations = obs_blocks.shape
    members = ensemble.shape[1]
    tiles = observations * members // (TILE_ROWS * TILE_COLS)
    per_x = tiles // (2 * nx)
    per_y = per_x // ny
    tile = (TILE_ROWS, TILE_COLS)
    one_batch = [
        pltpu.VMEM((2, tiles // 2, *tile), jnp.bfloat16),
        pltpu.VMEM((tiles // 2, *tile), jnp.bfloat16),
        pltpu.VMEM((nx - 1, per_x, *tile), jnp.bfloat16),
        pltpu.VMEM((ny - 1, per_y, *tile), jnp.bfloat16),
        pltpu.VMEM((nz - 1, per_y, *tile), jnp.bfloat16),
        pltpu.VMEM((per_y, *tile), jnp.bfloat16),
        pltpu.VMEM((2, nx, ny, per_y, *tile), jnp.bfloat16),
    ]
    copies = 2 * (1 + nx - 1 + ny - 1) + nz - 1
    vmem = pl.BlockSpec(memory_space=pltpu.VMEM)
    return pl.pallas_call(
        functools.partial(gather_kernel, nz, nx, ny),
        out_shape=jax.ShapeDtypeStruct((batches, observations, members), jnp.bfloat16),
        in_specs=[vmem] * 3,
        out_specs=vmem,
        scratch_shapes=one_batch * batches
        + [
            pltpu.SemaphoreType.DMA((batches, copies)),
            pltpu.SemaphoreType.DMA((batches, copies)),
        ],
        compiler_params=pltpu.CompilerParams(
            collective_id=0, has_side_effects=True, vmem_limit_bytes=32 * 1024 * 1024
        ),
        cost_estimate=pl.CostEstimate(flops=10**8, bytes_accessed=10**7, transcendentals=0),
        name="gather_observed",
    )(ensemble, obs_blocks, jnp.transpose(obs_weights, (0, 2, 1)))


PANEL, SUB = 32, 16

def parts_of(value, count):
    parts = []
    for _ in range(count):
        part = value.astype(jnp.bfloat16)
        parts.append(part)
        value = value - part.astype(jnp.float32)
    return parts

def factor_inverse(m_ref, t_ref):
    panel, sub = PANEL, SUB
    size = m_ref.shape[0]
    lanes = lax.broadcasted_iota(jnp.int32, (panel, 128), 1)
    rows_of = lax.broadcasted_iota(jnp.int32, (panel, 128), 0)
    rows8 = lax.broadcasted_iota(jnp.int32, (8, 128), 0)
    for start in range(0, size, panel):
        tile, lane0 = start // 128, start % 128
        here = pl.ds(start, panel)
        block = m_ref[here, tile * 128 : tile * 128 + 128]
        wide = []
        for t in range(size // 128):
            part = block if t == tile else m_ref[here, t * 128 : t * 128 + 128]
            if t == tile:
                inside = (lanes >= lane0) & (lanes < lane0 + panel)
                part = jnp.where(inside, jnp.where(lanes - lane0 == rows_of, 1.0, 0.0), part)
            wide.append(part)
        wide.append(block)
        done = [[] for _ in wide]
        scales = []
        top = 0
        for s in range(0, panel, sub):
            columns = {
                j: jnp.broadcast_to(wide[-1][:, lane0 + j : lane0 + j + 1], wide[-1].shape)
                for j in range(s, s + sub)
            }
            for k in range(s, s + sub):
                if k - top == 8:
                    for i, part in enumerate(wide):
                        done[i].append(part[:8])
                        wide[i] = part[8:]
                    columns = {j: c[8:] for j, c in columns.items() if j >= k}
                    top += 8
                at = k - top
                if at == 0:
                    scale = jnp.zeros((8, 128), jnp.float32)
                pivot = columns[k][at : at + 1]
                inverse = 1.0 / pivot
                scale = jnp.where(rows8 == at, lax.rsqrt(pivot), scale)
                below = rows_of[: panel - top] > at
                multiple = jnp.where(below, columns[k] * inverse, 0.0)
                for j in range(k + 1, s + sub):
                    columns[j] = columns[j] - multiple * columns[j][at : at + 1]
                last = len(wide) if s + sub < panel else len(wide) - 1
                for i in range(last):
                    wide[i] = wide[i] - multiple * wide[i][at : at + 1]
                if at == 7:
                    scales.append(scale)
        for i, part in enumerate(wide):
            done[i].append(part)
        scale = jnp.concatenate(scales, axis=0)
        scaled = [jnp.concatenate(done[i], axis=0) * scale for i in range(size // 128)]
        for t in range(size // 128):
            kept = scaled[t]
            if t == tile:
                kept = jnp.where(lanes < lane0 + panel, kept, 0.0)
            elif t > tile:
                kept = jnp.zeros_like(kept)
            t_ref[here, t * 128 : t * 128 + 128] = kept
        after = start + panel
        if after < size:
            first = after // 128
            whole = jnp.concatenate(scaled, axis=1)
            p = parts_of(whole, 3)
            left = [p[0], p[0], p[1], p[1], p[0], p[2]]
            right = [p[0], p[1], p[0], p[1], p[2], p[0]]
            left = jnp.concatenate(left, axis=0)[:, first * 128 :]
            right = jnp.concatenate(right, axis=0)
            product = lax.dot_general(
                left, right, (((0,), (0,)), ((), ())), preferred_element_type=jnp.float32
            )[after - first * 128 :]
            for t in range(size // 128):
                old = m_ref[after:, t * 128 : t * 128 + 128]
                if t == tile:
                    at_lane = lax.broadcasted_iota(jnp.int32, old.shape, 1)
                    old = jnp.where((at_lane >= lane0) & (at_lane < lane0 + panel), 0.0, old)
                m_ref[after:, t * 128 : t * 128 + 128] = old - product[:, t * 128 : t * 128 + 128]


def dot_nt(left, right):
    return lax.dot_general(
        left, right, (((1,), (1,)), ((), ())), preferred_element_type=jnp.float32
    )


def three_pass(dot, left, right):
    (left_high, left_low), (right_high, right_low) = left, right
    return dot(left_high, right_low) + dot(left_low, right_high) + dot(left_high, right_high)


def dot_nn(left, right):
    return jnp.dot(left, right, preferred_element_type=jnp.float32)


def analysis_kernel(
    raw_ref, state_ref, noise_ref, tags_ref, values_ref, out_ref, rows_ref, m_ref, t_ref
):
    local_rows, members = state_ref.shape
    batches, observations = tags_ref.shape
    variances = jnp.where(tags_ref[...] == 0, jnp.float32(0.5), jnp.float32(2.0))
    fill = jnp.zeros((8 - 2 * batches, observations), jnp.float32)
    by_row = jnp.concatenate([values_ref[...], jnp.sqrt(variances), fill], axis=0).T
    shape = (observations, observations)
    diagonal = lax.broadcasted_iota(jnp.int32, shape, 0) == lax.broadcasted_iota(
        jnp.int32, shape, 1
    )
    rows_ref[:local_rows] = state_ref[...]
    rows_ref[local_rows:] = raw_ref[1].astype(jnp.float32)
    for b in range(batches):
        if b == 0:
            observed = raw_ref[0].astype(jnp.float32)
        else:
            observed = rows_ref[local_rows:].astype(jnp.bfloat16).astype(jnp.float32)
        anomalies = split(observed - jnp.mean(observed, axis=1, keepdims=True))
        covariance = three_pass(dot_nt, anomalies, anomalies) * (1.0 / (members - 1))
        m_ref[...] = covariance + jnp.where(diagonal, variances[b : b + 1], 0.0)
        count = rows_ref.shape[0] if b + 1 < batches else local_rows
        rows = rows_ref[:count]
        centred = split(rows - jnp.mean(rows, axis=1, keepdims=True))
        product = split(three_pass(dot_nt, centred, anomalies) * (1.0 / (members - 1)))
        innovation = split(
            by_row[:, b : b + 1]
            + by_row[:, batches + b : batches + b + 1] * noise_ref[b].astype(jnp.float32)
            - observed
        )
        factor_inverse(m_ref, t_ref)
        inverse = split(t_ref[...])
        projected_high, projected_low = split(three_pass(dot_nt, product, inverse))
        white_innov = three_pass(dot_nn, inverse, innovation).astype(jnp.bfloat16)
        change = dot_nn(projected_low, white_innov) + dot_nn(projected_high, white_innov)
        if b + 1 < batches:
            rows_ref[:count] = rows + change
        else:
            out_ref[...] = rows + change


def analyse(raw, ensemble, obs_noise, comp_tags, obs_values):
    local_rows, members = ensemble.shape
    observations = comp_tags.shape[1]
    vmem = pl.BlockSpec(memory_space=pltpu.VMEM)
    square = pltpu.VMEM((observations, observations), jnp.float32)
    return pl.pallas_call(
        analysis_kernel,
        out_shape=jax.ShapeDtypeStruct(ensemble.shape, jnp.float32),
        in_specs=[vmem] * 5,
        out_specs=vmem,
        scratch_shapes=[
            pltpu.VMEM((local_rows + observations, members), jnp.float32),
            square,
            square,
        ],
        compiler_params=pltpu.CompilerParams(vmem_limit_bytes=48 * 1024 * 1024),
        cost_estimate=pl.CostEstimate(flops=10**10, bytes_accessed=10**7, transcendentals=0),
        name="analyse",
    )(raw, ensemble, obs_noise, comp_tags, obs_values)


def body(ensemble, obs_blocks, obs_weights, comp_tags, obs_values, obs_noise):
    raw = gather_observed(ensemble, obs_blocks, obs_weights)
    return analyse(raw, ensemble, obs_noise, comp_tags, obs_values)


def solution(mesh):
    in_specs = (P(("row", "col"), None), P(), P(), P(), P(), P())
    out_specs = P(("row", "col"), None)
    return jax.shard_map(body, mesh=mesh, in_specs=in_specs, out_specs=out_specs, check_vma=False)
```

profile of v0, /device:TPU:1, one launch (start us, length us, event | category | flops | bytes accessed | tf_op | source)
XLA Modules:
  0.0 74.7 jit_solution(7443504675229965442)
XLA Ops:
  0.0 0.0 copy-start
  0.0 1.0 %copy-done = f32[128,1024]{1,0:T(8,128)S(1)} copy-done((f32[128,1024]{1,0:T(8,128)S(1)}, f32[128,1024]{1,0:T(8,128)}, u32[]{:S(2)}) %copy-start) | copy-done | bytes 524312
  1.0 0.0 copy-start.2
  1.0 0.7 copy-done.2
  1.7 0.0 copy-start.3
  1.7 0.7 copy-done.3
  2.4 0.0 copy-start.1
  2.4 0.0 copy-start.4
  2.4 0.0 copy-start.5
  2.4 0.0 copy-start.6
  2.4 53.8 %gather_observed.1.raw_ref = bf16[2,256,1024]{2,1,0:T(8,128)(2,1)S(1)} custom-call(f32[128,1024]{1,0:T(8,128)S(1)} %copy-done, s32[2,256]{1,0:T(2,128)S(1)} %copy-done.3, f32[2,4,256]{2,1,0:T(4,128)S(1)} %bitcast.1), custom_call_target="tpu_custom_call" | custom-call | flops 100000000 | bytes 10000000 | tf_op jit(solution)/shard_map/gather_observed/pallas_call | solution.py:200
  56.3 0.0 copy-done.1
  56.3 0.0 copy-done.4
  56.3 0.0 copy-done.5
  56.3 0.0 copy-done.6
  56.3 18.4 %analyse.1 = f32[128,1024]{1,0:T(8,128)} custom-call(bf16[2,256,1024]{2,1,0:T(8,128)(2,1)S(1)} %gather_observed.1.raw_ref, f32[128,1024]{1,0:T(8,128)S(1)} %copy-done.1, bf16[2,256,1024]{2,1,0:T(8,128)(2,1)S(1)} %copy-done.4, s32[2,256]{1,0:T(2,128)S(1)} %copy-done.5, f32[2,256]{1,0:T(2,128)S(1)} %copy-done.6), custom_call_target="tpu_custom_call" | custom-call | flops 10000000000 | bytes 10000000 | tf_op jit(solution)/shard_map/analyse/pallas_call | solution.py:369
Async XLA Ops:
  0.0 1.0 %copy-start = (f32[128,1024]{1,0:T(8,128)S(1)}, f32[128,1024]{1,0:T(8,128)}, u32[]{:S(2)}) copy-start(f32[128,1024]{1,0:T(8,128)} %state_ref.3) | copy-start | bytes 1572868
  1.0 0.7 copy-start.2
  1.7 0.7 copy-start.3
  2.4 53.9 %copy-start.1 = (f32[128,1024]{1,0:T(8,128)S(1)}, f32[128,1024]{1,0:T(8,128)}, u32[]{:S(2)}) copy-start(f32[128,1024]{1,0:T(8,128)} %state_ref.3) | copy-start | bytes 1572868
  2.4 53.9 %copy-start.4 = (bf16[2,256,1024]{2,1,0:T(8,128)(2,1)S(1)}, bf16[2,256,1024]{2,1,0:T(8,128)(2,1)}, u32[]{:S(2)}) copy-start(bf16[2,256,1024]{2,1,0:T(8,128)(2,1)} %noise_ref.1) | copy-start | bytes 3145732
  2.4 53.9 %copy-start.5 = (s32[2,256]{1,0:T(2,128)S(1)}, s32[2,256]{1,0:T(2,128)}, u32[]{:S(2)}) copy-start(s32[2,256]{1,0:T(2,128)} %tags_ref.1) | copy-start | bytes 6148
  2.4 53.9 %copy-start.6 = (f32[2,256]{1,0:T(2,128)S(1)}, f32[2,256]{1,0:T(2,128)}, u32[]{:S(2)}) copy-start(f32[2,256]{1,0:T(2,128)} %values_ref.1) | copy-start | bytes 6148
where the time goes:
time: 75 us; the launch traced here: 74.7 us
  Pallas kernels  72.3 us (96%)
  local copies, waits for them, and re-layouts  2.43 us (3%)
    pallas_call x1, Pallas kernels, gather_observed(): pl.pallas_call(functools.partial(gather_kernel, nz, nx, ny), out_shape=ja...  53.8 us
    pallas_call x1, Pallas kernels, analyse(): pl.pallas_call(analysis_kernel, out_shape=jax.ShapeDtypeStruct(ensemble.s...  18.4 us
    unnamed x14, local copies, waits for them, and re-layouts  2.43 us

commit v1 on v0

--- a/solution.py
+++ b/solution.py
@@ -8,9 +8,14 @@
 from jax.sharding import PartitionSpec as P
 
 NX = 4
+PIECES = 4
 TILE_ROWS = 16
 TILE_COLS = 128
 MESH = pl.DeviceIdType.MESH
+
+
+def farthest_first(count):
+    return sorted(range(1, count), key=lambda d: -min(d, count - d))
 
 
 def split(value):
@@ -24,10 +29,26 @@
     )
 
 
-def gather_kernel(nz, nx, ny, state_ref, blocks_ref, weights_ref, out_ref, *scratch):
+def filter_kernel(nz, nx, ny, *refs):
+    hbm, out_ref, local = refs[:6], refs[6], refs[7:13]
+    rows_ref, raw_ref, m_ref, t_ref, load_sems, send_sems, recv_sems = refs[13:20]
+    y_relay, z_relay, scratch = refs[20:22], refs[22:25], refs[25:]
+    state_ref, blocks_ref, weights_ref, tags_ref, values_ref, noise_ref = local
     nb = blocks_ref.shape[0]
     batches = [scratch[7 * b : 7 * b + 7] for b in range(nb)]
-    send_sems, recv_sems = scratch[7 * nb :]
+    piece = state_ref.shape[0] // PIECES
+    pairs = [
+        (hbm[0].at[pl.ds(i * piece, piece)], state_ref.at[pl.ds(i * piece, piece)])
+        for i in range(PIECES)
+    ]
+    pairs = [*zip(hbm[1:3], local[1:3]), *pairs, *zip(hbm[3:], local[3:])]
+    loads = [
+        pltpu.make_async_copy(source, target, load_sems.at[i])
+        for i, (source, target) in enumerate(pairs)
+    ]
+    early, late = loads[: 2 + PIECES], loads[2 + PIECES :]
+    for load in early:
+        load.start()
     row = lax.axis_index("row")
     y = lax.axis_index("col")
     core = lax.rem(row, 2)
@@ -41,7 +62,23 @@
     x_peers = [place(z, lax.rem(x + d, nx), core, y) for d in range(1, nx)]
     y_peers = [place(z, x, core, lax.rem(y + d, ny)) for d in range(1, ny)]
     z_peers = [place(lax.rem(z + d, nz), x, core, y) for d in range(1, nz)]
-    peers = [core_peer, *x_peers, *y_peers, *z_peers]
+
+    def ring(peers, distance):
+        return (peers[distance - 1], peers[-distance])
+
+    peers = [core_peer, *x_peers, *ring(y_peers, 1), *ring(z_peers, 1)]
+
+    def tell(sem, targets):
+        for target in targets:
+            pl.semaphore_signal(sem, inc=1, device_id=target, device_id_type=MESH)
+
+    def meet_y():
+        pl.semaphore_wait(y_relay[0], 2)
+        tell(y_relay[1], ring(y_peers, 2))
+
+    def meet_z(step):
+        pl.semaphore_wait(z_relay[step], 2)
+        tell(z_relay[step + 1], ring(z_peers, 2))
 
     barrier = pltpu.get_barrier_semaphore()
     for peer in peers:
@@ -97,25 +134,25 @@
         if stage == 0:
             copies.append(copy(b, 0, part.at[1 - core], from_core, core_peer))
         elif stage == 1:
-            for d in range(1, nx):
+            for d in farthest_first(nx):
                 target = lax.rem(x + d, nx)
                 source = part.at[core, pl.ds(target * per_x, per_x)]
                 copies.append(copy(b, base[1] + d - 1, source, from_x.at[d - 1], x_peers[d - 1]))
         elif stage == 2:
-            for d in range(1, ny):
+            for d in farthest_first(ny):
                 target = lax.rem(y + d, ny)
                 source = part.at[core, pl.ds(x * per_x + target * per_y, per_y)]
                 copies.append(copy(b, base[2] + d - 1, source, from_y.at[d - 1], y_peers[d - 1]))
         elif stage == 3:
-            for d in range(1, nz):
+            for d in farthest_first(nz):
                 copies.append(copy(b, base[3] + d - 1, mine, from_z.at[d - 1], z_peers[d - 1]))
         elif stage == 4:
             whole = full.at[core, x, y]
-            for d in range(1, ny):
+            for d in farthest_first(ny):
                 copies.append(copy(b, base[4] + d - 1, whole, whole, y_peers[d - 1]))
         elif stage == 5:
             whole = full.at[core, x]
-            for d in range(1, nx):
+            for d in farthest_first(nx):
                 copies.append(copy(b, base[5] + d - 1, whole, whole, x_peers[d - 1]))
         else:
             whole = full.at[core]
@@ -147,36 +184,84 @@
 
     started = [[] for _ in range(nb)]
     current = [None] * nb
-    for b in range(nb):
-        interpolate(b)
-        if b == 0:
-            pl.semaphore_wait(barrier, len(peers))
-        current[b] = start_stage(b, 0)
+
+    def begin(b, stage):
+        current[b] = start_stage(b, stage)
         started[b] += current[b]
-    for stage in range(7):
-        for b in range(nb):
-            finish_stage(b, stage, current[b])
-            if stage < 6:
-                current[b] = start_stage(b, stage + 1)
-                started[b] += current[b]
-    for b in range(nb):
+
+    def advance(b, stage):
+        finish_stage(b, stage, current[b])
+        if stage < 6:
+            begin(b, stage + 1)
+
+    def assemble(b):
         full = batches[b][6]
-        columns = out_ref.shape[2] // TILE_COLS
-        for i in range(out_ref.shape[1] // TILE_ROWS):
+        columns = raw_ref.shape[2] // TILE_COLS
+        for i in range(raw_ref.shape[1] // TILE_ROWS):
             for j in range(columns):
                 tile = i * columns + j
                 c, rest = divmod(tile, nx * per_x)
                 x_, rest = divmod(rest, per_x)
                 y_, t = divmod(rest, per_y)
-                out_ref[
+                raw_ref[
                     b, i * TILE_ROWS : (i + 1) * TILE_ROWS, j * TILE_COLS : (j + 1) * TILE_COLS
                 ] = full[c, x_, y_, t]
+
+    for load in early:
+        load.wait()
+    for load in late:
+        load.start()
+    interpolate(0)
+    pl.semaphore_wait(barrier, len(peers))
+    tell(y_relay[0], ring(y_peers, 1))
+    tell(z_relay[0], ring(z_peers, 1))
+    begin(0, 0)
+    interpolate(1)
+    advance(0, 0)
+    begin(1, 0)
+    meet_y()
+    meet_z(0)
+    advance(1, 0)
+    pl.semaphore_wait(y_relay[1], 2)
+    advance(0, 1)
+    meet_z(1)
+    advance(1, 1)
+    pl.semaphore_wait(z_relay[2], 2)
+    for stage in range(2, 5):
+        advance(0, stage)
+        advance(1, stage)
+    advance(0, 5)
+    advance(0, 6)
+    assemble(0)
+    for load in late:
+        load.wait()
+
+    def receive():
+        advance(1, 5)
+
+    def receive_last():
+        advance(1, 6)
+        assemble(1)
+
+    analyse(
+        raw_ref,
+        state_ref,
+        noise_ref,
+        tags_ref,
+        values_ref,
+        out_ref,
+        rows_ref,
+        m_ref,
+        t_ref,
+        receive,
+        receive_last,
+    )
     for b in range(nb):
         for each in started[b]:
             each.wait_send()
 
 
-def gather_observed(ensemble, obs_blocks, obs_weights):
+def filter_call(ensemble, obs_blocks, obs_weights, comp_tags, obs_values, obs_noise):
     nx = NX
     ny = lax.axis_size("col")
     nz = lax.axis_size("row") // (2 * nx)
@@ -196,23 +281,32 @@
         pltpu.VMEM((2, nx, ny, per_y, *tile), jnp.bfloat16),
     ]
     copies = 2 * (1 + nx - 1 + ny - 1) + nz - 1
-    vmem = pl.BlockSpec(memory_space=pltpu.VMEM)
+    weights = jnp.transpose(obs_weights, (0, 2, 1))
+    operands = (ensemble, obs_blocks, weights, comp_tags, obs_values, obs_noise)
+    square = pltpu.VMEM((observations, observations), jnp.float32)
     return pl.pallas_call(
-        functools.partial(gather_kernel, nz, nx, ny),
-        out_shape=jax.ShapeDtypeStruct((batches, observations, members), jnp.bfloat16),
-        in_specs=[vmem] * 3,
-        out_specs=vmem,
-        scratch_shapes=one_batch * batches
+        functools.partial(filter_kernel, nz, nx, ny),
+        out_shape=jax.ShapeDtypeStruct(ensemble.shape, jnp.float32),
+        in_specs=[pl.BlockSpec(memory_space=pltpu.HBM)] * len(operands),
+        out_specs=pl.BlockSpec(memory_space=pltpu.VMEM),
+        scratch_shapes=[pltpu.VMEM(value.shape, value.dtype) for value in operands]
         + [
+            pltpu.VMEM((observations, members), jnp.float32),
+            pltpu.VMEM((batches, observations, members), jnp.bfloat16),
+            square,
+            square,
+            pltpu.SemaphoreType.DMA((len(operands) - 1 + PIECES,)),
             pltpu.SemaphoreType.DMA((batches, copies)),
             pltpu.SemaphoreType.DMA((batches, copies)),
-        ],
+        ]
+        + [pltpu.SemaphoreType.REGULAR] * 5
+        + one_batch * batches,
         compiler_params=pltpu.CompilerParams(
-            collective_id=0, has_side_effects=True, vmem_limit_bytes=32 * 1024 * 1024
+            collective_id=0, has_side_effects=True, vmem_limit_bytes=60 * 1024 * 1024
         ),
-        cost_estimate=pl.CostEstimate(flops=10**8, bytes_accessed=10**7, transcendentals=0),
-        name="gather_observed",
-    )(ensemble, obs_blocks, jnp.transpose(obs_weights, (0, 2, 1)))
+        cost_estimate=pl.CostEstimate(flops=10**10, bytes_accessed=10**7, transcendentals=0),
+        name="ensemble_filter",
+    )(*operands)
 
 
 PANEL, SUB = 32, 16
@@ -225,7 +319,7 @@
         value = value - part.astype(jnp.float32)
     return parts
 
-def factor_inverse(m_ref, t_ref):
+def factor_inverse(m_ref, t_ref, meanwhile):
     panel, sub = PANEL, SUB
     size = m_ref.shape[0]
     lanes = lax.broadcasted_iota(jnp.int32, (panel, 128), 1)
@@ -302,6 +396,7 @@
                     at_lane = lax.broadcasted_iota(jnp.int32, old.shape, 1)
                     old = jnp.where((at_lane >= lane0) & (at_lane < lane0 + panel), 0.0, old)
                 m_ref[after:, t * 128 : t * 128 + 128] = old - product[:, t * 128 : t * 128 + 128]
+            meanwhile(start // panel)
 
 
 def dot_nt(left, right):
@@ -319,11 +414,27 @@
     return jnp.dot(left, right, preferred_element_type=jnp.float32)
 
 
-def analysis_kernel(
-    raw_ref, state_ref, noise_ref, tags_ref, values_ref, out_ref, rows_ref, m_ref, t_ref
+def centre(value):
+    return split(value - jnp.mean(value, axis=1, keepdims=True))
+
+
+def analyse(
+    raw_ref,
+    state_ref,
+    noise_ref,
+    tags_ref,
+    values_ref,
+    out_ref,
+    pending_ref,
+    m_ref,
+    t_ref,
+    receive,
+    receive_last,
 ):
-    local_rows, members = state_ref.shape
+    members = state_ref.shape[1]
     batches, observations = tags_ref.shape
+    half = observations // 2
+    share = 1.0 / (members - 1)
     variances = jnp.where(tags_ref[...] == 0, jnp.float32(0.5), jnp.float32(2.0))
     fill = jnp.zeros((8 - 2 * batches, observations), jnp.float32)
     by_row = jnp.concatenate([values_ref[...], jnp.sqrt(variances), fill], axis=0).T
@@ -331,63 +442,78 @@
     diagonal = lax.broadcasted_iota(jnp.int32, shape, 0) == lax.broadcasted_iota(
         jnp.int32, shape, 1
     )
-    rows_ref[:local_rows] = state_ref[...]
-    rows_ref[local_rows:] = raw_ref[1].astype(jnp.float32)
+
+    def project(value, anomalies):
+        return split(three_pass(dot_nt, centre(value), anomalies) * share)
+
+    def columns(pair, start, stop):
+        return tuple(part[:, start:stop] for part in pair)
+
+    def rows(pair, start, stop):
+        return tuple(part[start:stop] for part in pair)
+
+    def change(projected, white_innov):
+        high, low = projected
+        return dot_nn(low, white_innov) + dot_nn(high, white_innov)
+
+    found = {}
     for b in range(batches):
         if b == 0:
             observed = raw_ref[0].astype(jnp.float32)
         else:
-            observed = rows_ref[local_rows:].astype(jnp.bfloat16).astype(jnp.float32)
-        anomalies = split(observed - jnp.mean(observed, axis=1, keepdims=True))
-        covariance = three_pass(dot_nt, anomalies, anomalies) * (1.0 / (members - 1))
+            observed = pending_ref[...].astype(jnp.bfloat16).astype(jnp.float32)
+        anomalies = centre(observed)
+        covariance = three_pass(dot_nt, anomalies, anomalies) * share
         m_ref[...] = covariance + jnp.where(diagonal, variances[b : b + 1], 0.0)
-        count = rows_ref.shape[0] if b + 1 < batches else local_rows
-        rows = rows_ref[:count]
-        centred = split(rows - jnp.mean(rows, axis=1, keepdims=True))
-        product = split(three_pass(dot_nt, centred, anomalies) * (1.0 / (members - 1)))
-        innovation = split(
-            by_row[:, b : b + 1]
-            + by_row[:, batches + b : batches + b + 1] * noise_ref[b].astype(jnp.float32)
-            - observed
-        )
-        factor_inverse(m_ref, t_ref)
-        inverse = split(t_ref[...])
-        projected_high, projected_low = split(three_pass(dot_nt, product, inverse))
-        white_innov = three_pass(dot_nn, inverse, innovation).astype(jnp.bfloat16)
-        change = dot_nn(projected_low, white_innov) + dot_nn(projected_high, white_innov)
+
+        def meanwhile(panel, b=b, observed=observed, anomalies=anomalies):
+            if panel == 0:
+                if b:
+                    state_ref[...] += change(*found["change"])
+                noise = noise_ref[b].astype(jnp.float32)
+                scale = by_row[:, batches + b : batches + b + 1]
+                found["innovation"] = split(by_row[:, b : b + 1] + scale * noise - observed)
+            elif panel == 1:
+                found["state"] = project(state_ref[...], anomalies)
+                if b == 0:
+                    receive()
+            elif panel == 3:
+                inverse = split(t_ref[:half, :half])
+                top = rows(found["innovation"], 0, half)
+                found["white"] = three_pass(dot_nn, inverse, top).astype(jnp.bfloat16)
+                found["top"] = inverse
+            elif panel == 4:
+                found["left"] = three_pass(
+                    dot_nt, columns(found["state"], 0, half), found["top"]
+                )
+                if b == 0:
+                    receive_last()
+                    found["pending"] = project(raw_ref[1].astype(jnp.float32), anomalies)
+            elif panel == 5 and b == 0:
+                found["pending_left"] = three_pass(
+                    dot_nt, columns(found["pending"], 0, half), found["top"]
+                )
+
+        factor_inverse(m_ref, t_ref, meanwhile)
+        inverse = split(t_ref[half:])
+        bottom = three_pass(dot_nn, inverse, found["innovation"]).astype(jnp.bfloat16)
+        white_innov = jnp.concatenate([found["white"], bottom], axis=0)
+
+        def projected(left, product):
+            right = three_pass(dot_nt, product, inverse)
+            return split(jnp.concatenate([left, right], axis=1))
+
         if b + 1 < batches:
-            rows_ref[:count] = rows + change
+            pending = projected(found["pending_left"], found["pending"])
+            pending_ref[...] = raw_ref[1].astype(jnp.float32) + change(pending, white_innov)
+            found["change"] = (projected(found["left"], found["state"]), white_innov)
         else:
-            out_ref[...] = rows + change
-
-
-def analyse(raw, ensemble, obs_noise, comp_tags, obs_values):
-    local_rows, members = ensemble.shape
-    observations = comp_tags.shape[1]
-    vmem = pl.BlockSpec(memory_space=pltpu.VMEM)
-    square = pltpu.VMEM((observations, observations), jnp.float32)
-    return pl.pallas_call(
-        analysis_kernel,
-        out_shape=jax.ShapeDtypeStruct(ensemble.shape, jnp.float32),
-        in_specs=[vmem] * 5,
-        out_specs=vmem,
-        scratch_shapes=[
-            pltpu.VMEM((local_rows + observations, members), jnp.float32),
-            square,
-            square,
-        ],
-        compiler_params=pltpu.CompilerParams(vmem_limit_bytes=48 * 1024 * 1024),
-        cost_estimate=pl.CostEstimate(flops=10**10, bytes_accessed=10**7, transcendentals=0),
-        name="analyse",
-    )(raw, ensemble, obs_noise, comp_tags, obs_values)
-
-
-def body(ensemble, obs_blocks, obs_weights, comp_tags, obs_values, obs_noise):
-    raw = gather_observed(ensemble, obs_blocks, obs_weights)
-    return analyse(raw, ensemble, obs_noise, comp_tags, obs_values)
+            out_ref[...] = state_ref[...] + change(
+                projected(found["left"], found["state"]), white_innov
+            )
 
 
 def solution(mesh):
     in_specs = (P(("row", "col"), None), P(), P(), P(), P(), P())
     out_specs = P(("row", "col"), None)
-    return jax.shard_map(body, mesh=mesh, in_specs=in_specs, out_specs=out_specs, check_vma=False)
+    return jax.shard_map(filter_call, mesh=mesh, in_specs=in_specs, out_specs=out_specs, check_vma=False)

time: 75 us -> 70 us (0.933)
  Pallas kernels: 72.3 us -> 67.9 us
    pallas_call x2 -> x1, Pallas kernels: 72.3 us -> 67.9 us  [filter_call(): pl.pallas_call(functools.partial(filter_kernel, nz, nx, ny), out_shape=ja...]
    unnamed x14 -> x1, local copies, waits for them, and re-layouts: 2.43 us -> 1.89 us
where the time goes in v1:
time: 70 us; the launch traced here: 69.8 us
  Pallas kernels  67.9 us (97%)
  local copies, waits for them, and re-layouts  1.89 us (3%)
    pallas_call x1, Pallas kernels, filter_call(): pl.pallas_call(functools.partial(filter_kernel, nz, nx, ny), out_shape=ja...  67.9 us
    unnamed x1, local copies, waits for them, and re-layouts  1.89 us

profile of v1, /device:TPU:1, one launch (start us, length us, event | category | flops | bytes accessed | tf_op | source)
XLA Modules:
  0.0 69.8 jit_solution(4821834146027580975)
XLA Ops:
  0.0 67.9 %ensemble_filter.1 = f32[128,1024]{1,0:T(8,128)} custom-call(f32[128,1024]{1,0:T(8,128)} %refs_0_.1, s32[2,256]{1,0:T(2,128)} %refs_1_.1, f32[2,4,256]{2,1,0:T(4,128)} %bitcast.1, s32[2,256]{1,0:T(2,128)} %refs_3_.1, f32[2,256]{1,0:T(2,128)} %refs_4_.1, bf16[2,256,1024]{2,1,0:T(8,128)(2,1)} %refs_5_.1), custom_call_target="tpu_custom_call" | custom-call | flops 10000000000 | bytes 10000000 | tf_op jit(solution)/shard_map/ensemble_filter/pallas_call | solution.py:287
  67.9 1.9 %copy.8 = f32[128,1024]{1,0:T(8,128)} copy(f32[128,1024]{1,0:T(8,128)} %ensemble_filter.1) | data formatting | bytes 1048576

commit v2 on v1

--- a/solution.py
+++ b/solution.py
@@ -30,9 +30,9 @@
 
 
 def filter_kernel(nz, nx, ny, *refs):
-    hbm, out_ref, local = refs[:6], refs[6], refs[7:13]
-    rows_ref, raw_ref, m_ref, t_ref, load_sems, send_sems, recv_sems = refs[13:20]
-    y_relay, z_relay, scratch = refs[20:22], refs[22:25], refs[25:]
+    hbm, out_hbm, local = refs[:6], refs[6], refs[7:13]
+    rows_ref, raw_ref, m_ref, t_ref, out_ref, load_sems, send_sems, recv_sems = refs[13:21]
+    y_relay, z_relay, scratch = refs[21:23], refs[23:26], refs[26:]
     state_ref, blocks_ref, weights_ref, tags_ref, values_ref, noise_ref = local
     nb = blocks_ref.shape[0]
     batches = [scratch[7 * b : 7 * b + 7] for b in range(nb)]
@@ -125,7 +125,7 @@
     per_x = batches[0][0].shape[1] // nx
     per_y = per_x // ny
     base = [0]
-    for count in (1, nx - 1, ny - 1, nz - 1, ny - 1, nx - 1, 1):
+    for count in (1, nx - 1, ny - 1, nz - 1, ny - 1, nx - 1, nx):
         base.append(base[-1] + count)
 
     def start_stage(b, stage):
@@ -155,16 +155,28 @@
             for d in farthest_first(nx):
                 copies.append(copy(b, base[5] + d - 1, whole, whole, x_peers[d - 1]))
         else:
-            whole = full.at[core]
-            copies.append(copy(b, base[6], whole, whole, core_peer))
+            copies = forwarded[b]
+            return copies
         for each in copies:
             each.start()
         return copies
 
+    forwarded = [[] for _ in range(nb)]
+
+    def forward(b, d):
+        chunk = batches[b][6].at[core, lax.rem(x + nx - d, nx)]
+        forwarded[b].append(copy(b, base[6] + d, chunk, chunk, core_peer))
+        forwarded[b][-1].start()
+
     def finish_stage(b, stage, copies):
         part, from_core, from_x, from_y, from_z, mine, full = batches[b]
+        for d, each in zip(farthest_first(nx)[::-1], copies[::-1]):
+            if stage == 5:
+                each.wait_recv()
+                forward(b, d)
         for each in copies:
-            each.wait_recv()
+            if stage != 5:
+                each.wait_recv()
         if stage == 0:
             part[core] = part[core] + from_core[...]
         elif stage == 1:
@@ -187,12 +199,20 @@
 
     def begin(b, stage):
         current[b] = start_stage(b, stage)
-        started[b] += current[b]
+        if stage == 5:
+            forward(b, 0)
+        started[b].append(current[b])
+
+    def settle(b, keep):
+        while len(started[b]) > keep:
+            for each in started[b].pop(0):
+                each.wait_send()
 
     def advance(b, stage):
         finish_stage(b, stage, current[b])
         if stage < 6:
             begin(b, stage + 1)
+            settle(b, 2)
 
     def assemble(b):
         full = batches[b][6]
@@ -216,8 +236,8 @@
     tell(y_relay[0], ring(y_peers, 1))
     tell(z_relay[0], ring(z_peers, 1))
     begin(0, 0)
+    advance(0, 0)
     interpolate(1)
-    advance(0, 0)
     begin(1, 0)
     meet_y()
     meet_z(0)
@@ -242,6 +262,8 @@
     def receive_last():
         advance(1, 6)
         assemble(1)
+        for b in range(nb):
+            settle(b, 0)
 
     analyse(
         raw_ref,
@@ -256,9 +278,18 @@
         receive,
         receive_last,
     )
-    for b in range(nb):
-        for each in started[b]:
-            each.wait_send()
+    stores = [
+        pltpu.make_async_copy(
+            out_ref.at[pl.ds(i * piece, piece)],
+            out_hbm.at[pl.ds(i * piece, piece)],
+            load_sems.at[i],
+        )
+        for i in range(PIECES)
+    ]
+    for store in stores:
+        store.start()
+    for store in stores:
+        store.wait()
 
 
 def filter_call(ensemble, obs_blocks, obs_weights, comp_tags, obs_values, obs_noise):
@@ -280,7 +311,7 @@
         pltpu.VMEM((per_y, *tile), jnp.bfloat16),
         pltpu.VMEM((2, nx, ny, per_y, *tile), jnp.bfloat16),
     ]
-    copies = 2 * (1 + nx - 1 + ny - 1) + nz - 1
+    copies = 2 * (nx + ny - 1) + nz - 1 + nx - 1
     weights = jnp.transpose(obs_weights, (0, 2, 1))
     operands = (ensemble, obs_blocks, weights, comp_tags, obs_values, obs_noise)
     square = pltpu.VMEM((observations, observations), jnp.float32)
@@ -288,13 +319,14 @@
         functools.partial(filter_kernel, nz, nx, ny),
         out_shape=jax.ShapeDtypeStruct(ensemble.shape, jnp.float32),
         in_specs=[pl.BlockSpec(memory_space=pltpu.HBM)] * len(operands),
-        out_specs=pl.BlockSpec(memory_space=pltpu.VMEM),
+        out_specs=pl.BlockSpec(memory_space=pltpu.HBM),
         scratch_shapes=[pltpu.VMEM(value.shape, value.dtype) for value in operands]
         + [
             pltpu.VMEM((observations, members), jnp.float32),
             pltpu.VMEM((batches, observations, members), jnp.bfloat16),
             square,
             square,
+            pltpu.VMEM(ensemble.shape, jnp.float32),
             pltpu.SemaphoreType.DMA((len(operands) - 1 + PIECES,)),
             pltpu.SemaphoreType.DMA((batches, copies)),
             pltpu.SemaphoreType.DMA((batches, copies)),
@@ -414,8 +446,8 @@
     return jnp.dot(left, right, preferred_element_type=jnp.float32)
 
 
-def centre(value):
-    return split(value - jnp.mean(value, axis=1, keepdims=True))
+def two_pass(dot, pair, exact):
+    return dot(pair[1], exact) + dot(pair[0], exact)
 
 
 def analyse(
@@ -436,81 +468,71 @@
     half = observations // 2
     share = 1.0 / (members - 1)
     variances = jnp.where(tags_ref[...] == 0, jnp.float32(0.5), jnp.float32(2.0))
-    fill = jnp.zeros((8 - 2 * batches, observations), jnp.float32)
-    by_row = jnp.concatenate([values_ref[...], jnp.sqrt(variances), fill], axis=0).T
+    scales = jnp.sqrt(variances)
     shape = (observations, observations)
     diagonal = lax.broadcasted_iota(jnp.int32, shape, 0) == lax.broadcasted_iota(
         jnp.int32, shape, 1
     )
 
-    def project(value, anomalies):
-        return split(three_pass(dot_nt, centre(value), anomalies) * share)
-
-    def columns(pair, start, stop):
-        return tuple(part[:, start:stop] for part in pair)
-
-    def rows(pair, start, stop):
-        return tuple(part[start:stop] for part in pair)
-
-    def change(projected, white_innov):
-        high, low = projected
-        return dot_nn(low, white_innov) + dot_nn(high, white_innov)
-
+    def rotate(product, inverse):
+        return split(three_pass(dot_nt, product, inverse))
+
+    state_split = split(state_ref[...])
     found = {}
     for b in range(batches):
-        if b == 0:
-            observed = raw_ref[0].astype(jnp.float32)
-        else:
-            observed = pending_ref[...].astype(jnp.bfloat16).astype(jnp.float32)
-        anomalies = centre(observed)
+        observed = raw_ref[0] if b == 0 else pending_ref[...].astype(jnp.bfloat16)
+        wide = observed.astype(jnp.float32)
+        anomalies = split(wide - jnp.mean(wide, axis=1, keepdims=True))
         covariance = three_pass(dot_nt, anomalies, anomalies) * share
         m_ref[...] = covariance + jnp.where(diagonal, variances[b : b + 1], 0.0)
 
-        def meanwhile(panel, b=b, observed=observed, anomalies=anomalies):
-            if panel == 0:
-                if b:
-                    state_ref[...] += change(*found["change"])
-                noise = noise_ref[b].astype(jnp.float32)
-                scale = by_row[:, batches + b : batches + b + 1]
-                found["innovation"] = split(by_row[:, b : b + 1] + scale * noise - observed)
+        def whiten(start, stop, b=b, observed=observed):
+            factor = t_ref[start:stop, :stop]
+            inverse = split(factor)
+            scaled = split(factor * scales[b : b + 1, :stop])
+            constant = jnp.sum(factor * values_ref[b : b + 1, :stop], axis=1, keepdims=True)
+            white_innov = (
+                two_pass(dot_nn, scaled, noise_ref[b, :stop])
+                - two_pass(dot_nn, inverse, observed[:stop])
+                + constant
+            )
+            return inverse, white_innov.astype(jnp.bfloat16)
+
+        def turn_top(name):
+            inverse, white_innov = found["top"]
+            turned = rotate(tuple(part[:, :half] for part in found[name]), inverse)
+            found[name + "_change"] = two_pass(dot_nn, turned, white_innov)
+
+        def meanwhile(panel, b=b, anomalies=anomalies):
+            if panel == 0 and b:
+                state_ref[...] += found["change"]
             elif panel == 1:
-                found["state"] = project(state_ref[...], anomalies)
-                if b == 0:
-                    receive()
+                pair = split(state_ref[...]) if b else state_split
+                found["state"] = split(three_pass(dot_nt, pair, anomalies) * share)
             elif panel == 3:
-                inverse = split(t_ref[:half, :half])
-                top = rows(found["innovation"], 0, half)
-                found["white"] = three_pass(dot_nn, inverse, top).astype(jnp.bfloat16)
-                found["top"] = inverse
-            elif panel == 4:
-                found["left"] = three_pass(
-                    dot_nt, columns(found["state"], 0, half), found["top"]
-                )
-                if b == 0:
-                    receive_last()
-                    found["pending"] = project(raw_ref[1].astype(jnp.float32), anomalies)
-            elif panel == 5 and b == 0:
-                found["pending_left"] = three_pass(
-                    dot_nt, columns(found["pending"], 0, half), found["top"]
-                )
+                found["top"] = whiten(0, half)
+            elif panel == 5:
+                turn_top("state")
+            if b == 0 and panel == 2:
+                receive()
+            if b == 0 and panel == 5:
+                receive_last()
+                product = dot_nt(raw_ref[1], anomalies[1]) + dot_nt(raw_ref[1], anomalies[0])
+                found["pending"] = split(product * share)
+                turn_top("pending")
 
         factor_inverse(m_ref, t_ref, meanwhile)
-        inverse = split(t_ref[half:])
-        bottom = three_pass(dot_nn, inverse, found["innovation"]).astype(jnp.bfloat16)
-        white_innov = jnp.concatenate([found["white"], bottom], axis=0)
-
-        def projected(left, product):
-            right = three_pass(dot_nt, product, inverse)
-            return split(jnp.concatenate([left, right], axis=1))
+        inverse, white_innov = whiten(half, observations)
+
+        def last_change(name):
+            turned = rotate(found[name], inverse)
+            return found[name + "_change"] + two_pass(dot_nn, turned, white_innov)
 
         if b + 1 < batches:
-            pending = projected(found["pending_left"], found["pending"])
-            pending_ref[...] = raw_ref[1].astype(jnp.float32) + change(pending, white_innov)
-            found["change"] = (projected(found["left"], found["state"]), white_innov)
+            pending_ref[...] = raw_ref[1].astype(jnp.float32) + last_change("pending")
+            found["change"] = last_change("state")
         else:
-            out_ref[...] = state_ref[...] + change(
-                projected(found["left"], found["state"]), white_innov
-            )
+            out_ref[...] = state_ref[...] + last_change("state")
 
 
 def solution(mesh):

time: 70 us -> 69 us (0.986)
  Pallas kernels: 67.9 us -> 66.9 us
    pallas_call x1, Pallas kernels: 67.9 us -> 66.9 us  [filter_call(): pl.pallas_call(functools.partial(filter_kernel, nz, nx, ny), out_shape=ja...]
where the time goes in v2:
time: 69 us; the launch traced here: 68.8 us
  Pallas kernels  66.9 us (97%)
  local copies, waits for them, and re-layouts  1.89 us (3%)
    pallas_call x1, Pallas kernels, filter_call(): pl.pallas_call(functools.partial(filter_kernel, nz, nx, ny), out_shape=ja...  66.9 us
    unnamed x1, local copies, waits for them, and re-layouts  1.89 us

profile of v2, /device:TPU:1, one launch (start us, length us, event | category | flops | bytes accessed | tf_op | source)
XLA Modules:
  0.0 68.8 jit_solution(14012559841352596825)
XLA Ops:
  0.0 66.9 %ensemble_filter.1 = f32[128,1024]{1,0:T(8,128)} custom-call(f32[128,1024]{1,0:T(8,128)} %refs_0_.1, s32[2,256]{1,0:T(2,128)} %refs_1_.1, f32[2,4,256]{2,1,0:T(4,128)} %bitcast.1, s32[2,256]{1,0:T(2,128)} %refs_3_.1, f32[2,256]{1,0:T(2,128)} %refs_4_.1, bf16[2,256,1024]{2,1,0:T(8,128)(2,1)} %refs_5_.1), custom_call_target="tpu_custom_call" | custom-call | flops 10000000000 | bytes 10000000 | tf_op jit(solution)/shard_map/ensemble_filter/pallas_call | solution.py:318
  66.9 1.9 %copy.8 = f32[128,1024]{1,0:T(8,128)} copy(f32[128,1024]{1,0:T(8,128)} %ensemble_filter.1) | data formatting | bytes 1048576
